TPU v7x, 32 devices: a whole 2x2x4 slice. The times are simulated.
32 devices in a mesh: sample: 8 (over y, x, core), slab: 4 (over z).
Axes of the slice: x: 2, y: 2, z: 4, core: 2. Of those that a mesh axis runs over, the one named last changes fastest.
Arguments:
- volume: bfloat16 [4, 8, 16, 4096], P(None, 'sample', 'slab'), may hold values from -6 to 6
- cotangent: bfloat16 [128, 8, 4, 256], P(None, 'sample', 'slab'), may hold values from -1.25 to 1.25
- w_first: bfloat16 [27, 4, 32], replicated, may hold values from -0.625 to 0.625
- b_first: float32 [32], replicated, may hold values from -3 to 3
- w_second: bfloat16 [27, 32, 64], replicated, may hold values from -0.21875 to 0.21875
- b_second: float32 [64], replicated, may hold values from -3 to 3
- w_third: bfloat16 [27, 64, 128], replicated, may hold values from -0.15625 to 0.15625
- b_third: float32 [128], replicated, may hold values from -3 to 3
Outputs:
- features: bfloat16 [128, 8, 4, 256], P(None, 'sample', 'slab')
- kernel_grad_first: float32 [27, 4, 32], replicated
- bias_grad_first: float32 [32], replicated
- kernel_grad_second: float32 [27, 32, 64], replicated
- bias_grad_second: float32 [64], replicated
- kernel_grad_third: float32 [27, 64, 128], replicated
- bias_grad_third: float32 [128], replicated
All inputs are finite; a program needn't handle non-finite values.
Results may differ from a plain program's by a relative error of at most 0.02.
Values may be sent and summed in bfloat16 or wider, within the bound.
A program may use at most 128 MiB of HBM per device.

v0:
```python
import jax
import jax.numpy as jnp
from jax import lax
from jax.sharding import PartitionSpec as P

SX = 32
CZ = 4


def with_halo(shard, sides, width):
    for axis, dim in sides:
        size, length = (lax.axis_size(axis), shard.shape[dim])
        up = [(i, (i + 1) % size) for i in range(size - 1)]
        down = [(j, i) for i, j in up]
        last = lax.slice_in_dim(shard, length - width, length, axis=dim)
        first = lax.slice_in_dim(shard, 0, width, axis=dim)
        before = lax.ppermute(last, axis, up)
        after = lax.ppermute(first, axis, down)
        shard = jnp.concatenate([before, shard, after], axis=dim)
    return shard


def silu_slope(values):
    sigmoid = jax.nn.sigmoid(values)
    return sigmoid * (1.0 + values * (1.0 - sigmoid))


def put_block(values, update, sample, depth_start):
    return lax.dynamic_update_slice(values, update, (0, sample, depth_start, 0))


def gather_taps(section, row_width):
    depth_len = section.shape[2] - 2
    plane_size = section.shape[3]
    flattened = jnp.pad(section, ((0, 0), (0, 0), (0, 0), (row_width + 1, row_width + 1)))
    column = lax.broadcasted_iota(jnp.int32, (1, 1, 1, plane_size), 3) % row_width
    left_mask = (column >= 1).astype(section.dtype)
    right_mask = (column <= row_width - 2).astype(section.dtype)
    pieces = []
    for tap_index in range(27):
        depth_start = tap_index // 9
        row_step = tap_index // 3 % 3 - 1
        col_step = tap_index % 3 - 1
        offset = row_width + 1 + row_step * row_width + col_step
        shifted = flattened[
            :, :, depth_start : depth_start + depth_len, offset : offset + plane_size
        ]
        if col_step < 0:
            shifted = shifted * left_mask
        elif col_step > 0:
            shifted = shifted * right_mask
        pieces.append(shifted)
    return jnp.concatenate(pieces, axis=0)


def apply_weight(patches, weight):
    flat_weight = weight.reshape(weight.shape[0] * weight.shape[1], weight.shape[2])
    return jnp.einsum("ko,kgzp->ogzp", flat_weight, patches, preferred_element_type=jnp.float32)


def weight_term(patches, grad_block, in_channels):
    summed = jnp.einsum("kgzp,ogzp->ko", patches, grad_block, preferred_element_type=jnp.float32)
    return summed.reshape(27, in_channels, grad_block.shape[0])


def pool_cells(values, row_width):
    channels, samples, depth_len, plane_size = values.shape
    row_count = plane_size // row_width
    grouped = values.reshape(
        channels, samples, depth_len // 2, 2, row_count // 2, 2, row_width // 2, 2
    )
    return grouped.mean(axis=(3, 5, 7)).reshape(channels, samples, depth_len // 2, plane_size // 4)


def spread_cells(values, coarse_width):
    channels, samples, depth_len, plane_size = values.shape
    row_count = plane_size // coarse_width
    grouped = values.reshape(channels, samples, depth_len, 1, row_count, 1, coarse_width, 1)
    grouped = jnp.broadcast_to(
        grouped, (channels, samples, depth_len, 2, row_count, 2, coarse_width, 2)
    )
    return grouped.reshape(channels, samples, 2 * depth_len, 4 * plane_size) * 0.125


def forward_layer(padded, weight, bias_values, row_width, depth_block, pooled_out):
    out_channels = weight.shape[2]
    samples, depth_total, plane_size = (padded.shape[1], padded.shape[2] - 2, padded.shape[3])
    per_sample = depth_total // depth_block
    pre_buffer = jnp.zeros((out_channels, samples, depth_total, plane_size), jnp.bfloat16)
    if pooled_out:
        out_buffer = jnp.zeros(
            (out_channels, samples, depth_total // 2, plane_size // 4), jnp.bfloat16
        )
    else:
        out_buffer = jnp.zeros_like(pre_buffer)

    def forward_block_step(block_index, buffers):
        sample = block_index // per_sample
        depth_start = block_index % per_sample * depth_block
        pre_values = (
            apply_weight(gather_taps(padded, row_width), weight) + bias_values[:, None, None, None]
        ).astype(jnp.bfloat16)
        activated = jax.nn.silu(pre_values.astype(jnp.float32))
        if pooled_out:
            result = put_block(
                buffers[1],
                pool_cells(activated, row_width).astype(jnp.bfloat16),
                sample,
                depth_start // 2,
            )
        else:
            result = put_block(buffers[1], activated.astype(jnp.bfloat16), sample, depth_start)
        return (put_block(buffers[0], pre_values, sample, depth_start), result)

    return lax.fori_loop(0, samples * per_sample, forward_block_step, (pre_buffer, out_buffer))


def weight_grads(padded, delta_values, row_width, depth_block, weight):
    samples, depth_total = (delta_values.shape[1], delta_values.shape[2])
    per_sample = depth_total // depth_block
    in_channels = weight.shape[1]

    def weight_block_step(block_index, summed):
        return summed + weight_term(gather_taps(padded, row_width), delta_values, in_channels)

    return lax.fori_loop(
        0, samples * per_sample, weight_block_step, jnp.zeros(weight.shape, jnp.float32)
    )


def data_grads(padded, flipped, row_width, depth_block):
    out_channels = flipped.shape[2]
    samples, depth_total, plane_size = (padded.shape[1], padded.shape[2] - 2, padded.shape[3])
    per_sample = depth_total // depth_block
    out_buffer = jnp.zeros((out_channels, samples, depth_total, plane_size), jnp.bfloat16)

    def data_block_step(block_index, buffer_now):
        sample = block_index // per_sample
        depth_start = block_index % per_sample * depth_block
        result = apply_weight(gather_taps(padded, row_width), flipped).astype(jnp.bfloat16)
        return put_block(buffer_now, result, sample, depth_start)

    return lax.fori_loop(0, samples * per_sample, data_block_step, out_buffer)


def bias_sum(delta_values):
    return jnp.sum(delta_values, axis=(1, 2, 3), dtype=jnp.float32)


def per_device(volume, cotangent, w_first, b_first, w_second, b_second, w_third, b_third):
    flipped_second = jnp.flip(w_second, 0).transpose(0, 2, 1)
    flipped_third = jnp.flip(w_third, 0).transpose(0, 2, 1)
    volume_padded = with_halo(volume, (("slab", 2),), 1)
    first_pre, first_pooled = forward_layer(volume_padded, w_first, b_first, SX, CZ, True)
    first_padded = with_halo(first_pooled, (("slab", 2),), 1)
    second_pre, second_pooled = forward_layer(
        first_padded, w_second, b_second, SX // 2, CZ // 2, True
    )
    coarse_depth = second_pooled.shape[2]
    third_padded = with_halo(second_pooled, (("slab", 2),), 1)
    third_pre, features = forward_layer(
        third_padded, w_third, b_third, SX // 4, coarse_depth, False
    )
    third_delta = (
        cotangent.astype(jnp.float32) * silu_slope(third_pre.astype(jnp.float32))
    ).astype(jnp.bfloat16)
    kernel_third = weight_grads(third_padded, third_delta, SX // 4, coarse_depth, w_third)
    bias_third = bias_sum(third_delta)
    kernel_third, bias_third = lax.psum((kernel_third, bias_third), ("sample", "slab"))
    delta_window = with_halo(third_delta, (("slab", 2),), 1)
    second_back = data_grads(delta_window, flipped_third, SX // 4, coarse_depth)
    second_delta = (
        spread_cells(second_back.astype(jnp.float32), SX // 4)
        * silu_slope(second_pre.astype(jnp.float32))
    ).astype(jnp.bfloat16)
    kernel_second = weight_grads(first_padded, second_delta, SX // 2, CZ // 2, w_second)
    bias_second = bias_sum(second_delta)
    delta_padded = with_halo(second_delta, (("slab", 2),), 1)
    first_back = data_grads(delta_padded, flipped_second, SX // 2, CZ // 2)
    first_delta = (
        spread_cells(first_back.astype(jnp.float32), SX // 2)
        * silu_slope(first_pre.astype(jnp.float32))
    ).astype(jnp.bfloat16)
    kernel_first = weight_grads(volume_padded, first_delta, SX, CZ, w_first)
    bias_first = bias_sum(first_delta)
    kernel_first, bias_first, kernel_second, bias_second = lax.psum(
        (kernel_first, bias_first, kernel_second, bias_second), ("sample", "slab")
    )
    return (
        features,
        kernel_first,
        bias_first,
        kernel_second,
        bias_second,
        kernel_third,
        bias_third,
    )


def solution(mesh):
    in_specs = (
        P(None, "sample", "slab", None),
        P(None, "sample", "slab", None),
        P(),
        P(),
        P(),
        P(),
        P(),
        P(),
    )
    out_specs = (P(None, "sample", "slab", None), P(), P(), P(), P(), P(), P())
    return jax.shard_map(
        per_device, mesh=mesh, in_specs=in_specs, out_specs=out_specs, check_vma=False
    )
```

profile of v0, /device:TPU:1, one launch (start us, length us, event | category | flops | bytes accessed | tf_op | source)
XLA Modules:
  0.0 260.9 jit_solution(14076122698188960177)
XLA Ops:
  7.2 1.0 copy.58
  8.3 4.0 %collective-permute-start = (bf16[4,1,1,4096]{3,0,2,1:T(4,128)(2,1)S(1)}, bf16[4,1,1,4096]{3,0,2,1:T(4,128)(2,1)S(1)}, u32[]{:S(2)}, u32[]{:S(2)}) collective-permute-start(bf16[4,1,1,4096]{3,0,2,1:T(4,128)(2,1)S(1)} %get-tuple-element.223), channel_id=1, source_target_pairs={{0,1},{1,2},{2,3},{4,5},{5,6},{6,7},{8,9},{9,10},{10,11},{12,13},{... | collective-permute-start | bytes 98312 | tf_op jit(solution)/shard_map/ppermute | solution.py:17
  12.3 1.3 collective-permute-start.1
  13.6 0.6 fusion.115
  14.2 0.9 reverse_bitcast_fusion.1
  15.2 1.0 reverse_bitcast_fusion
  16.2 1.4 reshape.324
  17.6 0.6 copy-done.3
  18.2 0.6 copy-done.5
  19.1 1.3 slice_multiply_fusion.36
  20.4 1.7 slice_multiply_fusion.37
  22.0 16.4 %concatenate.62 = bf16[108,1,4,4096]{3,0,2,1:T(8,128)(2,1)} concatenate(bf16[4,1,4,4096]{3,0,2,1:T(4,128)(2,1)} %get-tuple-element.212, bf16[4,1,4,4096]{3,0,2,1:T(4,128)(2,1)S(1)} %get-tuple-element.218, bf16[4,1,4,4096]{3,0,2,1:T(4,128)(2,1)S(1)} %get-tuple-element.203, bf16[4,1,4,4096]{3,0,2,1:T(4,128)(2,1)} %get-tuple-element.211, ...), dimensions={0} | concatenate | bytes 7077888 | tf_op jit(solution)/shard_map/while/body/eval_jaxpr/concatenate | solution.py:53
  38.4 4.7 %fusion.10 = (f32[32,4,4096]{2,0,1:T(8,128)S(1)}, f32[32,4,4096]{2,0,1:T(8,128)}) fusion(f32[32]{0:T(128)} %param.11, bf16[108,32]{1,0:T(8,128)(2,1)} %reshape.324, bf16[108,1,4,4096]{3,0,2,1:T(8,128)(2,1)} %concatenate.62), kind=kOutput, calls=%fused_computation.14 | convolution fusion | flops 116916224 | bytes 7740288 | tf_op jit(solution)/shard_map/while/body/eval_jaxpr/ko,kgzp->ogzp/dot_general | solution.py:58
  43.1 4.6 %copy.65 = f32[32,4,4096]{0,2,1:T(8,128)} copy(f32[32,4,4096]{2,0,1:T(8,128)S(1)} %get-tuple-element.225) | data formatting | bytes 4194304 | tf_op jit(solution)/shard_map/while/body/eval_jaxpr/jit(silu)/mul | solution.py:103
  47.7 9.5 %reduce_sum.54 = f32[32,2,64,16]{0,3,2,1:T(8,128)S(1)} reduce(f32[32,2,2,64,2,16,2]{0,6,5,4,3,2,1:T(2,128)} %bitcast.123, f32[]{:T(128)} %constant.224.clone.1), dimensions={2,4,6}, to_apply=%region_0.1 | reduce | flops 458752 | bytes 2359300 | tf_op jit(solution)/shard_map/while/body/eval_jaxpr/reduce_sum | solution.py:72
  57.6 4.0 %collective-permute-start.2 = (bf16[32,1,1,1024]{3,0,2,1:T(8,128)(2,1)S(1)}, bf16[32,1,1,1024]{3,0,2,1:T(8,128)(2,1)S(1)}, u32[]{:S(2)}, u32[]{:S(2)}) collective-permute-start(bf16[32,1,1,1024]{3,0,2,1:T(8,128)(2,1)S(1)} %get-tuple-element.219), channel_id=1, source_target_pairs={{0,1},{1,2},{2,3},{4,5},{5,6},{6,7},{8,9},{9,10},{10,11},{12,13},{... | collective-permute-start | bytes 196616 | tf_op jit(solution)/shard_map/ppermute | solution.py:17
  61.6 1.5 collective-permute-start.3
  63.1 3.5 %collective-permute-done.3 = bf16[32,1,1,1024]{3,0,2,1:T(8,128)(2,1)S(1)} collective-permute-done((bf16[32,1,1,1024]{3,0,2,1:T(8,128)(2,1)S(1)}, bf16[32,1,1,1024]{3,0,2,1:T(8,128)(2,1)S(1)}, u32[]{:S(2)}, u32[]{:S(2)}) %collective-permute-start.3) | collective-permute-done | bytes 65568 | tf_op jit(solution)/shard_map/ppermute | solution.py:18
  69.3 1.7 copy-done
  71.0 0.9 multiply_reduce_fusion
  72.1 0.4 reduce_sum.57
  72.6 1.3 collective-permute-start.5
  73.9 4.0 %collective-permute-start.4 = (bf16[64,1,1,256]{0,3,2,1:T(8,128)(2,1)S(1)}, bf16[64,1,1,256]{0,3,2,1:T(8,128)(2,1)S(1)}, u32[]{:S(2)}, u32[]{:S(2)}) collective-permute-start(bf16[64,1,1,256]{0,3,2,1:T(8,128)(2,1)S(1)} %fusion.106), channel_id=1, source_target_pairs={{0,1},{1,2},{2,3},{4,5},{5,6},{6,7},{8,9},{9,10},{10,11},{12,13},{... | collective-permute-start | bytes 98312 | tf_op jit(solution)/shard_map/ppermute | solution.py:17
  77.9 0.7 copy.75
  79.0 6.6 %copy.74 = bf16[108,4096,4]{1,2,0:T(4,128)(2,1)} copy(bf16[108,4096,4]{1,0,2:T(8,128)(2,1)} %bitcast.125) | data formatting | bytes 7077888 | tf_op jit(solution)/shard_map/while/body/eval_jaxpr/kgzp,ogzp->ko/dot_general | solution.py:62
  85.8 0.8 slice_multiply_fusion.72
  86.6 3.4 %concatenate.68 = bf16[1728,1,1,256]{0,3,2,1:T(8,128)(2,1)S(1)} concatenate(bf16[64,1,1,256]{0,3,2,1:T(8,128)(2,1)S(1)} %get-tuple-element.188, bf16[64,1,1,256]{0,3,2,1:T(8,128)(2,1)} %get-tuple-element.194, bf16[64,1,1,256]{0,3,2,1:T(8,128)(2,1)S(1)} %get-tuple-element.179, bf16[64,1,1,256]{0,3,2,1:T(8,128)(2,1)S(1)} %get-tuple-element.187, ...), dimensions={0} | concatenate | bytes 1769472 | tf_op jit(solution)/shard_map/while/body/eval_jaxpr/concatenate | solution.py:53
  90.0 0.6 copy.83
  90.6 1.4 convert_reduce_fusion.2
  92.1 1.3 collective-permute-start.7
  93.4 4.0 %collective-permute-start.6 = (bf16[128,1,1,256]{0,3,2,1:T(8,128)(2,1)S(1)}, bf16[128,1,1,256]{0,3,2,1:T(8,128)(2,1)S(1)}, u32[]{:S(2)}, u32[]{:S(2)}) collective-permute-start(bf16[128,1,1,256]{0,3,2,1:T(8,128)(2,1)S(1)} %get-tuple-element.156), channel_id=1, source_target_pairs={{0,1},{1,2},{2,3},{4,5},{5,6},{6,7},{8,9},{9,10},{10,11},{12,13},{... | collective-permute-start | bytes 196616 | tf_op jit(solution)/shard_map/ppermute | solution.py:17
  97.4 1.3 fusion.107
  98.7 0.7 copy.85
  102.0 0.7 fusion.53
  103.5 3.2 %collective-permute-start.8 = (bf16[64,1,1,1024]{3,0,2,1:T(8,128)(2,1)S(1)}, bf16[64,1,1,1024]{3,0,2,1:T(8,128)(2,1)S(1)}, u32[]{:S(2)}, u32[]{:S(2)}) collective-permute-start(bf16[64,1,1,1024]{3,0,2,1:T(8,128)(2,1)S(1)} %get-tuple-element.165), channel_id=1, source_target_pairs={{0,1},{1,2},{2,3},{4,5},{5,6},{6,7},{8,9},{9,10},{10,11},{12,13},{... | collective-permute-start | bytes 393224 | tf_op jit(solution)/shard_map/ppermute | solution.py:17
  106.7 1.5 collective-permute-start.9
  108.2 3.8 %convolution_bitcast_fusion = f32[27,32,64]{2,1,0:T(8,128)} fusion(bf16[27,32,1024,2]{2,1,0,3:T(8,128)(2,1)} %bitcast.131, bf16[64,2,1024]{2,0,1:T(8,128)(2,1)S(1)} %get-tuple-element.158), kind=kOutput, calls=%fused_computation.20 | convolution fusion | flops 226492416 | bytes 4022272 | tf_op jit(solution)/shard_map/while/body/eval_jaxpr/kgzp,ogzp->ko/dot_general | solution.py:62
  116.2 1.3 fusion.35
  117.5 0.3 copy.80
  117.8 7.5 %broadcast_in_dim.14 = f32[32,2,2,64,2,16,2]{0,6,5,4,3,2,1:T(2,128)} broadcast(f32[32,2,64,16]{0,3,2,1:T(8,128)S(1)} %bitcast.130), dimensions={0,1,3,5} | broadcast | bytes 2359296 | tf_op jit(solution)/shard_map/broadcast_in_dim | solution.py:79
  125.4 5.4 %copy.81 = f32[32,4,4096]{2,0,1:T(8,128)S(1)} copy(f32[32,4,4096]{0,2,1:T(8,128)} %bitcast.124) | data formatting | bytes 4194304 | tf_op jit(solution)/shard_map/mul | solution.py:82
  130.8 2.7 %convert_reduce_fusion = (f32[32]{0:T(128)S(1)}, bf16[32,4,4096]{2,0,1:T(8,128)(2,1)S(1)}) fusion(f32[32,4,4096]{2,0,1:T(8,128)S(1)} %copy.81, f32[32,4,4096]{2,0,1:T(8,128)} %get-tuple-element.226), kind=kLoop, calls=%fused_computation.11 | loop fusion | flops 5767136 | bytes 5243008 | tf_op jit(solution)/shard_map/reduce_sum | solution.py:147
  133.5 3.9 %fusion.41 = f32[27,4,32]{2,0,1:T(8,128)S(1)} fusion(bf16[27,4,4096,4]{2,3,1,0:T(4,128)(2,1)S(1)} %bitcast.133, bf16[32,4,4096]{2,0,1:T(8,128)(2,1)S(1)} %get-tuple-element.164), kind=kOutput, calls=%fused_computation.33 | convolution fusion | flops 113246208 | bytes 4601344 | tf_op jit(solution)/shard_map/while/body/eval_jaxpr/kgzp,ogzp->ko/dot_general | solution.py:62
  137.4 46.0 %all-reduce.5 = (f32[27,4,32]{2,0,1:T(8,128)S(1)}, f32[32]{0:T(128)}, f32[64]{0:T(128)}, f32[128]{0:T(128)}) all-reduce(f32[27,4,32]{2,0,1:T(8,128)S(1)} %fusion.41, f32[32]{0:T(128)S(1)} %get-tuple-element.159, f32[64]{0:T(128)S(1)} %get-tuple-element.157, ...), channel_id=1, replica_groups=mesh['sample'=8,'slab'=4] {'sample','slab'}, use_global_device_ids=true, to_apply=%region_3.4 | all-reduce | flops 3680 | bytes 29440 | tf_op jit(solution)/shard_map/psum | solution.py:186
  183.3 0.7 copy.86
  184.0 65.8 %all-reduce.9.cloned.1.call-done = (f32[27,32,64]{2,1,0:T(8,128)}, f32[27,64,128]{2,1,0:T(8,128)}) async-done(((f32[27,32,64]{2,1,0:T(8,128)}, f32[27,64,128]{2,1,0:T(8,128)}), (f32[27,32,64]{2,1,0:T(8,128)}, f32[27,64,128]{2,1,0:T(8,128)})) %all-reduce.9.cloned.1.call-update) | async-done | bytes 1105936 | tf_op jit(solution)/shard_map/psum | solution.py:186
  249.8 1.8 copy.184
  251.6 2.2 copy.185
  (136 shorter events, 10.9 us)
Async XLA Ops:
  7.2 242.7 %all-reduce.9.cloned.1.call-start = ((), (), s32[]{:S(2)}) async-start(), calls=%async_computation | async-start | bytes 2654208 | tf_op jit(solution)/shard_map/psum | solution.py:186
  8.3 9.4 %collective-permute-start = (bf16[4,1,1,4096]{3,0,2,1:T(4,128)(2,1)S(1)}, bf16[4,1,1,4096]{3,0,2,1:T(4,128)(2,1)S(1)}, u32[]{:S(2)}, u32[]{:S(2)}) collective-permute-start(bf16[4,1,1,4096]{3,0,2,1:T(4,128)(2,1)S(1)} %get-tuple-element.223), channel_id=1, source_target_pairs={{0,1},{1,2},{2,3},{4,5},{5,6},{6,7},{8,9},{9,10},{10,11},{12,13},{... | collective-permute-start | bytes 98312 | tf_op jit(solution)/shard_map/ppermute | solution.py:17
  12.3 5.3 %collective-permute-start.1 = (bf16[4,1,1,4096]{3,0,2,1:T(4,128)(2,1)S(1)}, bf16[4,1,1,4096]{3,0,2,1:T(4,128)(2,1)S(1)}, u32[]{:S(2)}, u32[]{:S(2)}) collective-permute-start(bf16[4,1,1,4096]{3,0,2,1:T(4,128)(2,1)S(1)} %get-tuple-element.224), channel_id=1, source_target_pairs={{1,0},{2,1},{3,2},{5,4},{6,5},{7,6},{9,8},{10,9},{11,10},{13,12},{... | collective-permute-start | bytes 98312 | tf_op jit(solution)/shard_map/ppermute | solution.py:18
  17.6 2.7 %copy-start.8 = (bf16[4096]{0:T(1024)(128)(2,1)S(1)}, bf16[4096]{0:T(1024)(128)(2,1)}, u32[]{:S(2)}) copy-start(bf16[4096]{0:T(1024)(128)(2,1)} %fusion.115) | copy-start | bytes 24580
  17.6 0.6 copy-start.3
  18.2 0.6 copy-start.5
  19.0 1.3 copy-start.4
  19.0 1.3 copy-start.6
  57.6 5.5 %collective-permute-start.2 = (bf16[32,1,1,1024]{3,0,2,1:T(8,128)(2,1)S(1)}, bf16[32,1,1,1024]{3,0,2,1:T(8,128)(2,1)S(1)}, u32[]{:S(2)}, u32[]{:S(2)}) collective-permute-start(bf16[32,1,1,1024]{3,0,2,1:T(8,128)(2,1)S(1)} %get-tuple-element.219), channel_id=1, source_target_pairs={{0,1},{1,2},{2,3},{4,5},{5,6},{6,7},{8,9},{9,10},{10,11},{12,13},{... | collective-permute-start | bytes 196616 | tf_op jit(solution)/shard_map/ppermute | solution.py:17
  61.6 5.0 %collective-permute-start.3 = (bf16[32,1,1,1024]{3,0,2,1:T(8,128)(2,1)S(1)}, bf16[32,1,1,1024]{3,0,2,1:T(8,128)(2,1)S(1)}, u32[]{:S(2)}, u32[]{:S(2)}) collective-permute-start(bf16[32,1,1,1024]{3,0,2,1:T(8,128)(2,1)S(1)} %get-tuple-element.220), channel_id=1, source_target_pairs={{1,0},{2,1},{3,2},{5,4},{6,5},{7,6},{9,8},{10,9},{11,10},{13,12},{... | collective-permute-start | bytes 196616 | tf_op jit(solution)/shard_map/ppermute | solution.py:18
  66.8 4.2 %copy-start.2 = (bf16[27,32,64]{2,1,0:T(8,128)(2,1)S(1)}, bf16[27,32,64]{2,1,0:T(8,128)(2,1)}, u32[]{:S(2)}) copy-start(bf16[27,32,64]{2,1,0:T(8,128)(2,1)} %param.12) | copy-start | bytes 331780
  66.8 4.2 %copy-start.9 = (f32[64]{0:T(128)S(1)}, f32[64]{0:T(128)}, u32[]{:S(2)}) copy-start(f32[64]{0:T(128)} %param.13) | copy-start | bytes 772
  69.3 1.7 copy-start
  71.0 6.9 %copy-start.7 = (bf16[128,1,1,256]{3,0,2,1:T(8,128)(2,1)S(1)}, bf16[128,1,1,256]{3,0,2,1:T(8,128)(2,1)}, u32[]{:S(2)}) copy-start(bf16[128,1,1,256]{3,0,2,1:T(8,128)(2,1)} %param.9) | copy-start | bytes 196612
  72.6 13.0 %collective-permute-start.5 = (bf16[64,1,1,256]{0,3,2,1:T(8,128)(2,1)S(1)}, bf16[64,1,1,256]{0,3,2,1:T(8,128)(2,1)S(1)}, u32[]{:S(2)}, u32[]{:S(2)}) collective-permute-start(bf16[64,1,1,256]{0,3,2,1:T(8,128)(2,1)S(1)} %fusion.106), channel_id=1, source_target_pairs={{1,0},{2,1},{3,2},{5,4},{6,5},{7,6},{9,8},{10,9},{11,10},{13,12},{... | collective-permute-start | bytes 98312 | tf_op jit(solution)/shard_map/ppermute | solution.py:18
  73.9 11.7 %collective-permute-start.4 = (bf16[64,1,1,256]{0,3,2,1:T(8,128)(2,1)S(1)}, bf16[64,1,1,256]{0,3,2,1:T(8,128)(2,1)S(1)}, u32[]{:S(2)}, u32[]{:S(2)}) collective-permute-start(bf16[64,1,1,256]{0,3,2,1:T(8,128)(2,1)S(1)} %fusion.106), channel_id=1, source_target_pairs={{0,1},{1,2},{2,3},{4,5},{5,6},{6,7},{8,9},{9,10},{10,11},{12,13},{... | collective-permute-start | bytes 98312 | tf_op jit(solution)/shard_map/ppermute | solution.py:17
  85.7 4.9 %copy-start.10 = (f32[128]{0:T(128)S(1)}, f32[128]{0:T(128)}, u32[]{:S(2)}) copy-start(f32[128]{0:T(128)} %param.15) | copy-start | bytes 1540
  92.1 7.4 %collective-permute-start.7 = (bf16[128,1,1,256]{0,3,2,1:T(8,128)(2,1)S(1)}, bf16[128,1,1,256]{0,3,2,1:T(8,128)(2,1)S(1)}, u32[]{:S(2)}, u32[]{:S(2)}) collective-permute-start(bf16[128,1,1,256]{0,3,2,1:T(8,128)(2,1)S(1)} %get-tuple-element.156), channel_id=1, source_target_pairs={{1,0},{2,1},{3,2},{5,4},{6,5},{7,6},{9,8},{10,9},{11,10},{13,12},{... | collective-permute-start | bytes 196616 | tf_op jit(solution)/shard_map/ppermute | solution.py:18
  93.4 6.1 %collective-permute-start.6 = (bf16[128,1,1,256]{0,3,2,1:T(8,128)(2,1)S(1)}, bf16[128,1,1,256]{0,3,2,1:T(8,128)(2,1)S(1)}, u32[]{:S(2)}, u32[]{:S(2)}) collective-permute-start(bf16[128,1,1,256]{0,3,2,1:T(8,128)(2,1)S(1)} %get-tuple-element.156), channel_id=1, source_target_pairs={{0,1},{1,2},{2,3},{4,5},{5,6},{6,7},{8,9},{9,10},{10,11},{12,13},{... | collective-permute-start | bytes 196616 | tf_op jit(solution)/shard_map/ppermute | solution.py:17
  103.5 8.6 %collective-permute-start.8 = (bf16[64,1,1,1024]{3,0,2,1:T(8,128)(2,1)S(1)}, bf16[64,1,1,1024]{3,0,2,1:T(8,128)(2,1)S(1)}, u32[]{:S(2)}, u32[]{:S(2)}) collective-permute-start(bf16[64,1,1,1024]{3,0,2,1:T(8,128)(2,1)S(1)} %get-tuple-element.165), channel_id=1, source_target_pairs={{0,1},{1,2},{2,3},{4,5},{5,6},{6,7},{8,9},{9,10},{10,11},{12,13},{... | collective-permute-start | bytes 393224 | tf_op jit(solution)/shard_map/ppermute | solution.py:17
  106.7 5.7 %collective-permute-start.9 = (bf16[64,1,1,1024]{3,0,2,1:T(8,128)(2,1)S(1)}, bf16[64,1,1,1024]{3,0,2,1:T(8,128)(2,1)S(1)}, u32[]{:S(2)}, u32[]{:S(2)}) collective-permute-start(bf16[64,1,1,1024]{3,0,2,1:T(8,128)(2,1)S(1)} %get-tuple-element.166), channel_id=1, source_target_pairs={{1,0},{2,1},{3,2},{5,4},{6,5},{7,6},{9,8},{10,9},{11,10},{13,12},{... | collective-permute-start | bytes 393224 | tf_op jit(solution)/shard_map/ppermute | solution.py:18
  130.8 2.7 %copy-start.1 = (bf16[108,4096,4]{1,2,0:T(4,128)(2,1)S(1)}, bf16[108,4096,4]{1,2,0:T(4,128)(2,1)}, u32[]{:S(2)}) copy-start(bf16[108,4096,4]{1,2,0:T(4,128)(2,1)} %copy.74) | copy-start | bytes 10616836
Sparse Core Ops, SparseCore 0:
  112.2 137.6 all-reduce.8
where the time goes:
time: 265 us; the launch traced here: 261 us
  waiting for transfers between devices  69.7 us (26%)
  local copies, waits for them, and re-layouts  61.3 us (23%)
  blocking collectives  46 us (17%)
  starting transfers between devices  26.1 us (10%)
  other arithmetic  24.5 us (9%)
  matrix products  18 us (7%)
  between operations  15.3 us (6%)
    psum x1, waiting for transfers between devices, per_device(): lax.psum((kernel_first, bias_first, kernel_second, bias_second), ('sample...  65.8 us
    psum x1, blocking collectives, per_device(): lax.psum((kernel_first, bias_first, kernel_second, bias_second), ('sample...  46 us
    concatenate x3, local copies, waits for them, and re-layouts, gather_taps(): return jnp.concatenate(pieces, axis=0)  20.4 us
    ppermute x5, starting transfers between devices, with_halo(): before = lax.ppermute(last, axis, up)  19.2 us
    unnamed x52, local copies, waits for them, and re-layouts  12.9 us
    reduce_sum x2, other arithmetic, pool_cells(): grouped.mean(axis=(3, 5, 7))  9.96 us
    dot_general x3, matrix products, weight_term(): jnp.einsum('kgzp,ogzp->ko', patches, grad_block, preferred_element_type=j...  9.02 us
    dot_general x5, matrix products, apply_weight(): jnp.einsum('ko,kgzp->ogzp', flat_weight, patches, preferred_element_type=...  9 us
  transfers between devices with their start and end apart: 11, of which 3 were waited for; matrix products, arithmetic and copies ran while one was open for 16% of the time, Pallas kernels for 0%

commit v1 on v0

v1 whole, which is shorter than its diff:
```python
import functools

import jax
import jax.numpy as jnp
import numpy as np
from jax import lax
from jax.experimental import pallas as pl
from jax.experimental.pallas import tpu as pltpu
from jax.sharding import PartitionSpec as P

SY, SX = 32, 8
CELLS = SY * SX
F32, BF16 = jnp.float32, jnp.bfloat16
NT = (((1,), (1,)), ((), ()))
PLANE = 144
ROW_B3, ROW_G2, ROW_B2, ROW_G1, ROW_B1, ROWS = 1728, 1744, 2176, 2192, 2320, 2352


def selection():
    sel = np.zeros((PLANE, 288), np.float32)
    for y in range(6):
        for x in range(6):
            sy, y4 = divmod(y - 1, 4)
            sx, x4 = divmod(x - 1, 4)
            if sy < 0:
                base = (sx + 1) * 16 + x4 * 4
            elif sy == 0:
                base = 48 + (sx + 1) * 64 + y4 * 16 + x4 * 4
            else:
                base = 240 + (sx + 1) * 16 + x4 * 4
            for c in range(4):
                sel[(y * 6 + x) * 4 + c, base + c] = 1.0
    return sel


def dot(a, b):
    return jnp.dot(a, b, preferred_element_type=F32)


def dot_nt(a, b):
    return lax.dot_general(a, b, NT, preferred_element_type=F32)


def shifter():
    lane = lax.broadcasted_iota(jnp.int32, (1, CELLS), 1)
    row, column = lane // SX, lane % SX

    def shift(values, sy, sx):
        if sy == 0 and sx == 0:
            return values
        moved = pltpu.roll(values, (-(sy * SX + sx)) % CELLS, 1)
        keep = None
        for coordinate, size, step in ((row, SY, sy), (column, SX, sx)):
            if step != 0:
                inside = coordinate > 0 if step < 0 else coordinate < size - 1
                keep = inside if keep is None else keep & inside
        return jnp.where(keep, moved, 0.0)

    return shift


def activation(values):
    sigmoid = 1.0 / (1.0 + jnp.exp(-values))
    return values * sigmoid, sigmoid * (1.0 + values * (1.0 - sigmoid))


PHASES = [(a, b) for a in range(2) for b in range(2)]
TAPS = [(i, j, k) for i in range(3) for j in range(3) for k in range(3)]


def network_kernel(
    slabs, v_ref, cot_ref, sel_ref, w1_ref, b1_ref, w2_ref, b2_ref, w3_ref, b3_ref, w2f_ref,
    w3f_ref, feat_ref, pack_ref, rv, rf, rs, rd3, rd2, f1, f2, d3, d2, stack, a1, w1b, slope1,
    p2, slope2, s3, s3d, p2d, send_sem, recv_sem,
):
    me = lax.axis_index("slab")
    has_prev, has_next = me > 0, me < slabs - 1
    shift = shifter()

    barrier = pltpu.get_barrier_semaphore()
    for there, peer in ((has_prev, me - 1), (has_next, me + 1)):

        @pl.when(there)
        def _():
            pl.semaphore_signal(
                barrier, inc=1, device_id={"slab": peer}, device_id_type=pl.DeviceIdType.MESH
            )

    @pl.when(has_prev & has_next)
    def _():
        pl.semaphore_wait(barrier, 2)

    @pl.when(~(has_prev & has_next))
    def _():
        pl.semaphore_wait(barrier, 1)

    def copies(index, up_src, down_src, landing):
        up = pltpu.make_async_remote_copy(
            src_ref=up_src, dst_ref=landing.at[0], send_sem=send_sem.at[index, 0],
            recv_sem=recv_sem.at[index, 0], device_id={"slab": me + 1},
            device_id_type=pl.DeviceIdType.MESH,
        )
        down = pltpu.make_async_remote_copy(
            src_ref=down_src, dst_ref=landing.at[1], send_sem=send_sem.at[index, 1],
            recv_sem=recv_sem.at[index, 1], device_id={"slab": me - 1},
            device_id_type=pl.DeviceIdType.MESH,
        )
        return up, down

    def start(pair):
        @pl.when(has_next)
        def _():
            pair[0].start()

        @pl.when(has_prev)
        def _():
            pair[1].start()

    def arrive(pair, landing):
        @pl.when(has_prev)
        def _():
            pair[0].wait_recv()

        @pl.when(me == 0)
        def _():
            landing[0] = jnp.zeros(landing.shape[1:], landing.dtype)

        @pl.when(has_next)
        def _():
            pair[1].wait_recv()

        @pl.when(me == slabs - 1)
        def _():
            landing[1] = jnp.zeros(landing.shape[1:], landing.dtype)

    halo_v = copies(0, v_ref.at[3], v_ref.at[0], rv)
    start(halo_v)
    w1_wide = w1_ref[...]
    for index in range(16):
        (qy, qx), (py, px) = PHASES[index // 4], PHASES[index % 4]
        offset = ((2 * qy + py) * 6 + 2 * qx + px) * 4
        wide = w1_wide if offset == 0 else pltpu.roll(w1_wide, offset, 1)
        w1b[index * 32 : (index + 1) * 32, :] = wide.astype(BF16)
    bias_one = jnp.concatenate([b1_ref[...]] * 16, axis=0)
    a1[6 * PLANE :, :] = jnp.zeros((a1.shape[0] - 6 * PLANE, CELLS), BF16)

    def build_plane(z, plane):
        values = plane.astype(F32)
        row = 0
        for sy, lo, hi in ((-1, 48, 64), (0, 0, 64), (1, 0, 16)):
            for sx in (-1, 0, 1):
                stack[row : row + hi - lo, :] = shift(values[lo:hi], sy, sx).astype(BF16)
                row += hi - lo
        a1[z * PLANE : (z + 1) * PLANE, :] = dot(sel_ref[...], stack[...]).astype(BF16)

    def first_layer(z):
        pre = dot(w1b[:, : 3 * PLANE], a1[z * PLANE : (z + 3) * PLANE, :]) + bias_one
        active, slope = activation(pre.astype(BF16).astype(F32))
        slope1[z] = slope * 0.125
        parts = []
        for q in range(4):
            block = active[q * 128 : (q + 1) * 128]
            parts.append(block[0:32] + block[32:64] + block[64:96] + block[96:128])
        return parts

    for z in range(4):
        build_plane(z + 1, v_ref[z])
    part1, part2 = first_layer(1), first_layer(2)
    arrive(halo_v, rv)
    build_plane(0, rv[0])
    build_plane(5, rv[1])
    part0, part3 = first_layer(0), first_layer(3)
    for q in range(4):
        f1[0, q * 32 : (q + 1) * 32, :] = ((part0[q] + part1[q]) * 0.125).astype(BF16)
        f1[1, q * 32 : (q + 1) * 32, :] = ((part2[q] + part3[q]) * 0.125).astype(BF16)

    halo_f = copies(1, f1.at[1], f1.at[0], rf)
    start(halo_f)

    def spread_block(target, block, channels, place, flipped):
        for tap_index, (i, j, k) in enumerate(TAPS):
            steps = (2 - i, 2 - j, 2 - k) if flipped else (i, j, k)
            phase = [position - step for position, step in zip(place, steps)]
            if all(0 <= value <= 1 for value in phase):
                lane = (phase[0] * 4 + phase[1] * 2 + phase[2]) * CELLS
                target[
                    tap_index * channels : (tap_index + 1) * channels, lane : lane + CELLS
                ] = block

    def place_plane(target, take, channels, z, flipped):
        for y in range(4):
            sy, qy = divmod(y - 1, 2)
            for x in range(4):
                sx, qx = divmod(x - 1, 2)
                block = take(qy * 2 + qx)
                if sy != 0 or sx != 0:
                    block = shift(block.astype(F32), sy, sx).astype(BF16)
                spread_block(target, block, channels, (z, y, x), flipped)

    for z in range(2):
        place_plane(p2, lambda q: f1[z, q * 32 : (q + 1) * 32, :], 32, z + 1, False)
    arrive(halo_f, rf)
    for side, z in ((0, 0), (1, 3)):
        place_plane(p2, lambda q: rf[side, q * 32 : (q + 1) * 32, :], 32, z, False)
    pooled = jnp.zeros((64, CELLS), F32)
    for half in range(2):
        lanes = slice(half * 1024, (half + 1) * 1024)
        pre = dot(w2_ref[...], p2[:, lanes]) + b2_ref[...]
        active, slope = activation(pre.astype(BF16).astype(F32))
        slope2[:, lanes] = slope * 0.125
        for q in range(4):
            pooled = pooled + active[:, q * CELLS : (q + 1) * CELLS]
    f2[...] = (pooled * 0.125).astype(BF16)

    halo_s = copies(2, f2, f2, rs)
    start(halo_s)

    def place_coarse(target, plane, channels, i, flipped):
        values = plane.astype(F32)
        for j in range(3):
            for k in range(3):
                sy, sx = (1 - j, 1 - k) if flipped else (j - 1, k - 1)
                row = ((i * 3 + j) * 3 + k) * channels
                target[row : row + channels, :] = shift(values, sy, sx).astype(BF16)

    place_coarse(s3, f2[...], 64, 1, False)
    arrive(halo_s, rs)
    place_coarse(s3, rs[0], 64, 0, False)
    place_coarse(s3, rs[1], 64, 2, False)
    pre = dot(w3_ref[...], s3[...]) + b3_ref[...]
    active, slope = activation(pre.astype(BF16).astype(F32))
    feat_ref[...] = active.astype(BF16)
    d3[...] = (cot_ref[...].astype(F32) * slope).astype(BF16)

    halo_d3 = copies(3, d3, d3, rd3)
    start(halo_d3)
    pack_ref[0:ROW_B3, :] = dot_nt(s3[...], d3[...]).astype(BF16)
    pack_ref[ROW_B3:ROW_G2, :] = dot_nt(jnp.ones((16, CELLS), BF16), d3[...]).astype(BF16)
    place_coarse(s3d, d3[...], 128, 1, True)
    arrive(halo_d3, rd3)
    place_coarse(s3d, rd3[1], 128, 0, True)
    place_coarse(s3d, rd3[0], 128, 2, True)
    back = dot(w3f_ref[...], s3d[...]).astype(BF16).astype(F32)
    for p in range(8):
        d2[p // 4, :, p % 4 * CELLS : (p % 4 + 1) * CELLS] = (
            back * slope2[:, p * CELLS : (p + 1) * CELLS]
        ).astype(BF16)

    halo_d2 = copies(4, d2.at[1], d2.at[0], rd2)
    start(halo_d2)
    grad2 = dot_nt(p2[:, :1024], d2[0]) + dot_nt(p2[:, 1024:], d2[1])
    pack_ref[ROW_G2:ROW_B2, :] = jnp.concatenate([grad2[:432], grad2[432:]], axis=1).astype(BF16)
    ones = jnp.ones((16, 1024), BF16)
    sum2 = dot_nt(ones, d2[0]) + dot_nt(ones, d2[1])
    pack_ref[ROW_B2:ROW_G1, :] = jnp.concatenate([sum2, sum2], axis=1).astype(BF16)
    for z in range(2):
        place_plane(
            p2d, lambda q: d2[z, :, q * CELLS : (q + 1) * CELLS], 64, z + 1, True
        )
    arrive(halo_d2, rd2)
    for side, z in ((0, 0), (1, 3)):
        place_plane(
            p2d, lambda q: rd2[side, :, q * CELLS : (q + 1) * CELLS], 64, z, True
        )
    first_back = dot(w2f_ref[...], p2d[...]).astype(BF16).astype(F32)
    grad1 = jnp.zeros((512, 512), F32)
    sum1 = jnp.zeros((32, CELLS), F32)
    for z in range(4):
        blocks = []
        for index in range(16):
            lane = ((z // 2) * 4 + index // 4) * CELLS
            delta = (
                first_back[:, lane : lane + CELLS] * slope1[z, index * 32 : (index + 1) * 32, :]
            ).astype(BF16)
            sum1 = sum1 + delta.astype(F32)
            blocks.append(delta)
        delta = jnp.concatenate(blocks, axis=0)
        grad1 = grad1 + dot_nt(delta, a1[z * PLANE : z * PLANE + 512, :])
    folded = jnp.zeros((32, 512), F32)
    for index in range(16):
        (qy, qx), (py, px) = PHASES[index // 4], PHASES[index % 4]
        offset = ((2 * qy + py) * 6 + 2 * qx + px) * 4
        rows = grad1[index * 32 : (index + 1) * 32]
        folded = folded + (rows if offset == 0 else pltpu.roll(rows, 512 - offset, 1))
    for q in range(4):
        pack_ref[ROW_G1 + q * 32 : ROW_G1 + (q + 1) * 32, :] = folded[
            :, q * 128 : (q + 1) * 128
        ].astype(BF16)
    total = jnp.sum(sum1, axis=1, keepdims=True)
    pack_ref[ROW_B1:ROWS, :] = jnp.broadcast_to(total, (32, 128)).astype(BF16)
    pack_ref[ROWS:, :] = jnp.zeros((pack_ref.shape[0] - ROWS, 128), BF16)

    for pair in (halo_v, halo_f, halo_s, halo_d3, halo_d2):

        @pl.when(has_next)
        def _():
            pair[0].wait_send()

        @pl.when(has_prev)
        def _():
            pair[1].wait_send()


def sum_kernel(
    samples, slabs, pack_ref, out_ref, land_a, land_b, part, whole, send_a, recv_a, send_b,
    recv_b, send_c, recv_c, send_d, recv_d,
):
    s, z = lax.axis_index("sample"), lax.axis_index("slab")
    chunk = pack_ref.shape[0] // samples
    piece = chunk // slabs
    mesh_id = pl.DeviceIdType.MESH
    sample_peers = [lax.rem(s + k, samples) for k in range(1, samples)]
    slab_peers = [lax.rem(z + k, slabs) for k in range(1, slabs)]

    barrier = pltpu.get_barrier_semaphore()
    for axis, peers in (("sample", sample_peers), ("slab", slab_peers)):
        for peer in peers:
            pl.semaphore_signal(barrier, inc=1, device_id={axis: peer}, device_id_type=mesh_id)
    pl.semaphore_wait(barrier, samples + slabs - 2)

    def rows(start, size):
        return pl.ds(pl.multiple_of(start, 16), size)

    def exchange(axis, peers, mine, source, target, arrival, send, recv):
        for peer in peers:
            pltpu.make_async_remote_copy(
                src_ref=source(peer), dst_ref=target, send_sem=send.at[peer],
                recv_sem=recv.at[mine], device_id={axis: peer}, device_id_type=mesh_id,
            ).start()

        def settle(peer):
            pltpu.make_async_remote_copy(
                src_ref=source(peer), dst_ref=arrival(peer), send_sem=send.at[peer],
                recv_sem=recv.at[peer], device_id={axis: peer}, device_id_type=mesh_id,
            ).wait()

        return settle

    settle = exchange(
        "sample", sample_peers, s, lambda peer: pack_ref.at[rows(peer * chunk, chunk)],
        land_a.at[s], lambda peer: land_a.at[peer], send_a, recv_a,
    )
    total = pack_ref[rows(s * chunk, chunk), :].astype(F32)
    for peer in sample_peers:
        settle(peer)
        total = total + land_a[peer].astype(F32)
    part[...] = total.astype(BF16)

    settle = exchange(
        "slab", slab_peers, z, lambda peer: part.at[rows(peer * piece, piece)],
        land_b.at[z], lambda peer: land_b.at[peer], send_b, recv_b,
    )
    total = part[rows(z * piece, piece), :].astype(F32)
    for peer in slab_peers:
        settle(peer)
        total = total + land_b[peer].astype(F32)
    own = rows(s * chunk + z * piece, piece)
    whole[own, :] = total.astype(BF16)

    settle = exchange(
        "slab", slab_peers, z, lambda peer: whole.at[own], whole.at[own],
        lambda peer: whole.at[rows(s * chunk + peer * piece, piece)], send_c, recv_c,
    )
    for peer in slab_peers:
        settle(peer)
    band = rows(s * chunk, chunk)
    settle = exchange(
        "sample", sample_peers, s, lambda peer: whole.at[band], whole.at[band],
        lambda peer: whole.at[rows(peer * chunk, chunk)], send_d, recv_d,
    )
    out_ref[band, :] = whole[band, :].astype(F32)
    for peer in sample_peers:
        settle(peer)
        out_ref[rows(peer * chunk, chunk), :] = whole[rows(peer * chunk, chunk), :].astype(F32)


def per_device(volume, cotangent, w_first, b_first, w_second, b_second, w_third, b_third):
    samples, slabs = lax.axis_size("sample"), lax.axis_size("slab")
    unit = 16 * samples * slabs
    pack_rows = -(-ROWS // unit) * unit
    vmem = pl.BlockSpec(memory_space=pltpu.VMEM)

    phased = volume.reshape(4, 4, SY, 4, SX, 4).transpose(1, 3, 5, 0, 2, 4).reshape(4, 64, CELLS)
    w1 = jnp.pad(
        w_first.astype(F32).reshape(3, 3, 3, 4, 32), ((0, 0), (0, 3), (0, 3), (0, 0), (0, 0))
    )
    w1 = jnp.pad(w1.reshape(3 * PLANE, 32).T, ((0, 0), (0, 512 - 3 * PLANE)))
    w2 = w_second.reshape(27 * 32, 64).T
    w3 = w_third.reshape(27 * 64, 128).T
    w2f = w_second.transpose(1, 0, 2).reshape(32, 27 * 64)
    w3f = w_third.transpose(1, 0, 2).reshape(64, 27 * 128)

    features, pack = pl.pallas_call(
        functools.partial(network_kernel, slabs),
        out_shape=(
            jax.ShapeDtypeStruct((128, CELLS), BF16),
            jax.ShapeDtypeStruct((pack_rows, 128), BF16),
        ),
        in_specs=[vmem] * 11,
        out_specs=(vmem, vmem),
        scratch_shapes=[
            pltpu.VMEM((2, 64, CELLS), BF16),
            pltpu.VMEM((2, 128, CELLS), BF16),
            pltpu.VMEM((2, 64, CELLS), BF16),
            pltpu.VMEM((2, 128, CELLS), BF16),
            pltpu.VMEM((2, 64, 4 * CELLS), BF16),
            pltpu.VMEM((2, 128, CELLS), BF16),
            pltpu.VMEM((64, CELLS), BF16),
            pltpu.VMEM((128, CELLS), BF16),
            pltpu.VMEM((2, 64, 4 * CELLS), BF16),
            pltpu.VMEM((288, CELLS), BF16),
            pltpu.VMEM((944, CELLS), BF16),
            pltpu.VMEM((512, 512), BF16),
            pltpu.VMEM((4, 512, CELLS), F32),
            pltpu.VMEM((864, 8 * CELLS), BF16),
            pltpu.VMEM((64, 8 * CELLS), F32),
            pltpu.VMEM((1728, CELLS), BF16),
            pltpu.VMEM((3456, CELLS), BF16),
            pltpu.VMEM((1728, 8 * CELLS), BF16),
            pltpu.SemaphoreType.DMA((5, 2)),
            pltpu.SemaphoreType.DMA((5, 2)),
        ],
        compiler_params=pltpu.CompilerParams(
            collective_id=0, has_side_effects=True, vmem_limit_bytes=48 * 2**20
        ),
        name="network",
    )(
        phased, cotangent.reshape(128, CELLS), jnp.asarray(selection(), BF16), w1,
        b_first[:, None], w2, b_second[:, None], w3, b_third[:, None], w2f, w3f,
    )

    chunk = pack_rows // samples
    summed = pl.pallas_call(
        functools.partial(sum_kernel, samples, slabs),
        out_shape=jax.ShapeDtypeStruct((pack_rows, 128), F32),
        in_specs=[vmem],
        out_specs=vmem,
        scratch_shapes=[
            pltpu.VMEM((samples, chunk, 128), BF16),
            pltpu.VMEM((slabs, chunk // slabs, 128), BF16),
            pltpu.VMEM((chunk, 128), BF16),
            pltpu.VMEM((pack_rows, 128), BF16),
        ]
        + [pltpu.SemaphoreType.DMA((n,)) for n in (samples, samples, slabs, slabs) * 1]
        + [pltpu.SemaphoreType.DMA((n,)) for n in (slabs, slabs, samples, samples)],
        compiler_params=pltpu.CompilerParams(
            collective_id=1, has_side_effects=True, vmem_limit_bytes=32 * 2**20
        ),
        name="sum_all",
    )(pack)

    kernel_third = summed[:ROW_B3].reshape(27, 64, 128)
    bias_third = summed[ROW_B3]
    grad2 = summed[ROW_G2:ROW_B2]
    kernel_second = jnp.concatenate([grad2[:, :64], grad2[:, 64:]], axis=0).reshape(27, 32, 64)
    bias_second = summed[ROW_B2, :64]
    grad1 = summed[ROW_G1:ROW_B1].reshape(4, 32, 128).transpose(1, 0, 2).reshape(32, 512)
    grad1 = grad1[:, : 3 * PLANE].reshape(32, 3, 6, 6, 4)[:, :, :3, :3, :]
    kernel_first = grad1.transpose(1, 2, 3, 4, 0).reshape(27, 4, 32)
    bias_first = summed[ROW_B1:ROWS, 0]
    return (
        features.reshape(128, 1, 1, CELLS),
        kernel_first,
        bias_first,
        kernel_second,
        bias_second,
        kernel_third,
        bias_third,
    )


def solution(mesh):
    split = P(None, "sample", "slab", None)
    in_specs = (split, split, P(), P(), P(), P(), P(), P())
    out_specs = (split, P(), P(), P(), P(), P(), P())
    return jax.shard_map(
        per_device, mesh=mesh, in_specs=in_specs, out_specs=out_specs, check_vma=False
    )
```

time: 265 us -> 92.1 us (0.35); the launches traced: 261 us -> 91.8 us
  waiting for transfers between devices: 69.7 us -> 0 us
  Pallas kernels: 0 us -> 53.8 us
  blocking collectives: 46 us -> 0 us
  starting transfers between devices: 26.1 us -> 0 us
  local copies, waits for them, and re-layouts: 61.3 us -> 36.4 us
  other arithmetic: 24.5 us -> 0.81 us
  matrix products: 18 us -> 0 us
  between operations: 15.3 us -> 0.84 us
    psum x1 -> x0, waiting for transfers between devices: 65.8 us -> none  [per_device(): lax.psum((kernel_first, bias_first, kernel_second, bias_second), ('sample...]
    pallas_call x0 -> x2, Pallas kernels: none -> 53.8 us  [the longest x1 32.5 us: per_device(): pl.pallas_call(functools.partial(sum_kernel, samples, slabs), out_shape=j...]
    psum x1 -> x0, blocking collectives: 46 us -> none  [per_device(): lax.psum((kernel_first, bias_first, kernel_second, bias_second), ('sample...]
    ppermute x10 -> x0, starting transfers between devices: 26.1 us -> none  [the longest x5 19.2 us: with_halo(): before = lax.ppermute(last, axis, up)]
    concatenate x3 -> x0, local copies, waits for them, and re-layouts: 20.4 us -> none  [gather_taps(): return jnp.concatenate(pieces, axis=0)]
    dot_general x8 -> x0, matrix products: 18 us -> none  [the longest x3 9.02 us: weight_term(): jnp.einsum('kgzp,ogzp->ko', patches, grad_block, preferred_element_type=j...]
    transpose x2, local copies, waits for them, and re-layouts: 1.04 us -> 16.4 us  [the longest x1 16.3 us: per_device(): volume.reshape(4, 4, SY, 4, SX, 4).transpose(1, 3, 5, 0, 2, 4)]
    reshape x2 -> x8, local copies, waits for them, and re-layouts: 1.62 us -> 15.5 us  [the longest x2 13.7 us: per_device(): volume.reshape(4, 4, SY, 4, SX, 4).transpose(1, 3, 5, 0, 2, 4)]
  transfers between devices with their start and end apart: 11 -> 0, of which waited for: 3 -> 0; matrix products, arithmetic and copies ran while one was open for 16% -> 0% of each run, Pallas kernels for 0% -> 0%
where the time goes in v1:
time: 92.1 us; the launch traced here: 91.8 us
  Pallas kernels  53.8 us (58%)
  local copies, waits for them, and re-layouts  36.4 us (40%)
    pallas_call x1, Pallas kernels, per_device(): pl.pallas_call(functools.partial(sum_kernel, samples, slabs), out_shape=j...  32.5 us
    pallas_call x1, Pallas kernels, per_device(): pl.pallas_call(functools.partial(network_kernel, slabs), out_shape=(jax.S...  21.3 us
    transpose x1, local copies, waits for them, and re-layouts, per_device(): volume.reshape(4, 4, SY, 4, SX, 4).transpose(1, 3, 5, 0, 2, 4)  16.3 us
    reshape x2, local copies, waits for them, and re-layouts, per_device(): volume.reshape(4, 4, SY, 4, SX, 4).transpose(1, 3, 5, 0, 2, 4)  13.7 us

profile of v1, /device:TPU:1, one launch (start us, length us, event | category | flops | bytes accessed | tf_op | source)
XLA Modules:
  0.0 91.8 jit_solution(1692837997943335088)
XLA Ops:
  0.6 10.7 %reshape.64 = bf16[4,4,32,4,8,4]{5,4,3,2,1,0:T(8,128)(2,1)} reshape(bf16[4,1,4,4096]{3,2,1,0:T(4,128)(2,1)} %param.9) | data formatting | bytes 262144 | tf_op jit(solution)/shard_map/reshape | solution.py:383
  11.3 16.3 %copy.36 = bf16[4,4,4,4,32,8]{5,4,3,2,1,0:T(8,128)(2,1)S(1)} copy(bf16[4,4,4,4,32,8]{2,5,1,4,0,3:T(8,128)(2,1)} %bitcast.43) | data formatting | bytes 262144 | tf_op jit(solution)/shard_map/transpose | solution.py:383
  27.6 0.0 copy-start.2
  27.6 2.9 %reshape.65.v_ref = bf16[4,64,256]{2,1,0:T(8,128)(2,1)S(1)} reshape(bf16[4,4,4,4,32,8]{5,4,3,2,1,0:T(8,128)(2,1)S(1)} %copy.36) | data formatting | bytes 262144 | tf_op jit(solution)/shard_map/reshape | solution.py:383
  30.6 0.0 copy-start.3
  30.6 0.0 copy-done.2
  30.6 0.0 copy-start.4
  30.6 0.2 copy.39
  30.9 0.0 copy-start.5
  30.9 0.0 copy-start.6
  30.9 0.0 copy-start.7
  30.9 0.0 copy-start
  30.9 0.0 copy-start.1
  30.9 1.1 %copy_bitcast_fusion.w3f_ref = bf16[64,3456]{1,0:T(8,128)(2,1)S(1)} fusion(bf16[27,64,128]{2,1,0:T(8,128)(2,1)} %param.15), kind=kLoop, calls=%fused_computation | loop fusion | bytes 884736 | tf_op jit(solution)/shard_map/reshape | solution.py:391
  32.0 0.0 copy-done.3
  32.0 0.1 copy.40
  32.1 0.2 reshape.71.w2f_ref
  32.4 0.0 copy-done.4
  32.4 0.1 copy.37
  32.6 0.1 copy.38
  32.7 0.0 copy-done.5
  32.7 0.1 copy.44.b3_ref
  32.8 0.0 copy-done.6
  32.8 0.1 copy.43.b2_ref
  32.9 0.0 copy-done.7
  32.9 0.1 copy.42.b1_ref
  33.0 0.0 copy-done
  33.0 0.0 copy-done.1
  33.0 21.3 %network.1 = (bf16[128,256]{1,0:T(8,128)(2,1)S(1)}, bf16[2560,128]{1,0:T(8,128)(2,1)S(1)}) custom-call(bf16[4,64,256]{2,1,0:T(8,128)(2,1)S(1)} %reshape.65.v_ref, bf16[128,256]{1,0:T(8,128)(2,1)S(1)} %bitcast.41, bf16[144,288]{1,0:T(8,128)(2,1)S(1)} %copy-done, f32[32,512]{1,0:T(8,128)S(1)} %pad_convert_fusion.w1_ref, f32[32,1]{1,0:T(8,128)S(1)} %copy.42.b1_ref, ...), custom_call_target="tpu_custom_call" | custom-call | tf_op jit(solution)/shard_map/network/pallas_call | solution.py:393
  54.3 32.5 %sum_all.1 = f32[2560,128]{1,0:T(8,128)S(1)} custom-call(bf16[2560,128]{1,0:T(8,128)(2,1)S(1)} %get-tuple-element.10.pack_ref), custom_call_target="tpu_custom_call" | custom-call | tf_op jit(solution)/shard_map/sum_all/pallas_call | solution.py:433
  86.8 0.1 fusion
  87.0 0.8 pad_maximum_fusion
  87.8 1.0 %slice.37 = f32[1728,128]{1,0:T(8,128)} slice(f32[2560,128]{1,0:T(8,128)S(1)} %sum_all.1), slice={[0:1728], [0:128]} | slice | bytes 1769472 | tf_op jit(solution)/shard_map/slice | solution.py:452
  88.8 0.1 copy.46
  88.9 0.6 slice.40
  89.6 0.5 slice_bitcast_fusion
  90.1 0.5 slice_bitcast_fusion.1
  90.6 0.6 slice_reduce_fusion
  91.2 0.6 copy.53
  (5 shorter events, 0.1 us)
Async XLA Ops:
  27.6 3.0 %copy-start.2 = (bf16[27,64,128]{2,1,0:T(8,128)(2,1)S(1)}, bf16[27,64,128]{2,1,0:T(8,128)(2,1)}, u32[]{:S(2)}) copy-start(bf16[27,64,128]{2,1,0:T(8,128)(2,1)} %param.15) | copy-start | bytes 1327108
  30.6 1.4 %copy-start.3 = (bf16[27,32,64]{2,1,0:T(8,128)(2,1)S(1)}, bf16[27,32,64]{2,1,0:T(8,128)(2,1)}, u32[]{:S(2)}) copy-start(bf16[27,32,64]{2,1,0:T(8,128)(2,1)} %param.13) | copy-start | bytes 331780
  30.6 1.8 %copy-start.4 = (bf16[27,4,32]{2,1,0:T(4,128)(2,1)S(1)}, bf16[27,4,32]{2,1,0:T(4,128)(2,1)}, u32[]{:S(2)}) copy-start(bf16[27,4,32]{2,1,0:T(4,128)(2,1)} %param.11) | copy-start | bytes 20740
  30.9 1.8 %copy-start.5 = (f32[128]{0:T(128)S(1)}, f32[128]{0:T(128)}, u32[]{:S(2)}) copy-start(f32[128]{0:T(128)} %param.16) | copy-start | bytes 1540
  30.9 2.0 %copy-start.6 = (f32[64]{0:T(128)S(1)}, f32[64]{0:T(128)}, u32[]{:S(2)}) copy-start(f32[64]{0:T(128)} %param.14) | copy-start | bytes 772
  30.9 2.0 %copy-start.7 = (f32[32]{0:T(128)S(1)}, f32[32]{0:T(128)}, u32[]{:S(2)}) copy-start(f32[32]{0:T(128)} %param.12) | copy-start | bytes 388
  30.9 2.1 %copy-start = (bf16[144,288]{1,0:T(8,128)(2,1)S(1)}, bf16[144,288]{1,0:T(8,128)(2,1)}, u32[]{:S(2)}) copy-start(bf16[144,288]{1,0:T(8,128)(2,1)} %constant.6.clone.sel_ref) | copy-start | bytes 248836
  30.9 2.1 %copy-start.1 = (bf16[128,1,1,256]{3,0,2,1:T(8,128)(2,1)S(1)}, bf16[128,1,1,256]{3,0,2,1:T(8,128)(2,1)}, u32[]{:S(2)}) copy-start(bf16[128,1,1,256]{3,0,2,1:T(8,128)(2,1)} %param.10) | copy-start | bytes 196612

commit v2 on v1

--- a/solution.py
+++ b/solution.py
@@ -33,6 +33,24 @@
     return sel
 
 
+def phase_spread():
+    out = np.zeros((128, 16, SY, SX), np.float32)
+    for y in range(4):
+        for x in range(4):
+            for column in range(SX):
+                out[y * 4 * SX + column * 4 + x, y * 4 + x, :, column] = 1.0
+    return out.reshape(128, 16 * CELLS)
+
+
+def plane_order():
+    out = np.zeros((256, 256), np.float32)
+    for phase in range(16):
+        for c in range(4):
+            for z in range(4):
+                out[z * 64 + phase * 4 + c, phase * 16 + c * 4 + z] = 1.0
+    return out
+
+
 def dot(a, b):
     return jnp.dot(a, b, preferred_element_type=F32)
 
@@ -69,8 +87,8 @@
 
 
 def network_kernel(
-    slabs, v_ref, cot_ref, sel_ref, w1_ref, b1_ref, w2_ref, b2_ref, w3_ref, b3_ref, w2f_ref,
-    w3f_ref, feat_ref, pack_ref, rv, rf, rs, rd3, rd2, f1, f2, d3, d2, stack, a1, w1b, slope1,
+    slabs, vol_ref, cot_ref, sel_ref, spread_ref, order_ref, w1_ref, b1_ref, w2_ref, b2_ref, w3_ref, b3_ref, w2f_ref,
+    w3f_ref, feat_ref, pack_ref, v_ref, rows_ref, rv, rf, rs, rd3, rd2, f1, f2, d3, d2, stack, a1, w1b, slope1,
     p2, slope2, s3, s3d, p2d, send_sem, recv_sem,
 ):
     me = lax.axis_index("slab")
@@ -133,6 +151,19 @@
         def _():
             landing[1] = jnp.zeros(landing.shape[1:], landing.dtype)
 
+    for row in range(SY):
+        rows_ref[row * 16 : (row + 1) * 16, :] = vol_ref[:, row * 128 : (row + 1) * 128]
+    own_row = lax.broadcasted_iota(jnp.int32, (1, CELLS), 1) // SX
+    phases = []
+    for phase in range(16):
+        spread = dot(rows_ref[...], spread_ref[:, phase * CELLS : (phase + 1) * CELLS])
+        picked = spread[0:16]
+        for row in range(1, SY):
+            picked = jnp.where(own_row == row, spread[row * 16 : (row + 1) * 16], picked)
+        phases.append(picked.astype(BF16))
+    ordered = dot(order_ref[...], jnp.concatenate(phases, axis=0)).astype(BF16)
+    for z in range(4):
+        v_ref[z] = ordered[z * 64 : (z + 1) * 64]
     halo_v = copies(0, v_ref.at[3], v_ref.at[0], rv)
     start(halo_v)
     w1_wide = w1_ref[...]
@@ -302,7 +333,7 @@
 
 
 def sum_kernel(
-    samples, slabs, pack_ref, out_ref, land_a, land_b, part, whole, send_a, recv_a, send_b,
+    samples, slabs, pack_ref, k1_ref, b1_ref, k2_ref, b2_ref, k3_ref, b3_ref, land_a, land_b, part, whole, turned, send_a, recv_a, send_b,
     recv_b, send_c, recv_c, send_d, recv_d,
 ):
     s, z = lax.axis_index("sample"), lax.axis_index("slab")
@@ -368,10 +399,22 @@
         "sample", sample_peers, s, lambda peer: whole.at[band], whole.at[band],
         lambda peer: whole.at[rows(peer * chunk, chunk)], send_d, recv_d,
     )
-    out_ref[band, :] = whole[band, :].astype(F32)
     for peer in sample_peers:
         settle(peer)
-        out_ref[rows(peer * chunk, chunk), :] = whole[rows(peer * chunk, chunk), :].astype(F32)
+    k3_ref[...] = whole[0:ROW_B3, :].astype(F32)
+    b3_ref[...] = whole[ROW_B3:ROW_G2, :].astype(F32)[0:1]
+    grad2 = whole[ROW_G2:ROW_B2, :].astype(F32)
+    k2_ref[0:432, :] = grad2[:, :64]
+    k2_ref[432:864, :] = grad2[:, 64:]
+    b2_ref[...] = whole[ROW_B2:ROW_G1, :].astype(F32)[0:1, :64]
+    for i in range(4):
+        block = whole[ROW_G1 + i * 32 : ROW_G1 + (i + 1) * 32, :].astype(F32)
+        turned[i * 128 : (i + 1) * 128, :] = block.T
+    for i in range(3):
+        for j in range(3):
+            row = i * PLANE + j * 24
+            k1_ref[(i * 3 + j) * 12 : (i * 3 + j + 1) * 12, :] = turned[row : row + 12, :]
+    b1_ref[...] = whole[ROW_B1:ROWS, :].astype(F32).T[0:1, :]
 
 
 def per_device(volume, cotangent, w_first, b_first, w_second, b_second, w_third, b_third):
@@ -380,7 +423,6 @@
     pack_rows = -(-ROWS // unit) * unit
     vmem = pl.BlockSpec(memory_space=pltpu.VMEM)
 
-    phased = volume.reshape(4, 4, SY, 4, SX, 4).transpose(1, 3, 5, 0, 2, 4).reshape(4, 64, CELLS)
     w1 = jnp.pad(
         w_first.astype(F32).reshape(3, 3, 3, 4, 32), ((0, 0), (0, 3), (0, 3), (0, 0), (0, 0))
     )
@@ -396,9 +438,11 @@
             jax.ShapeDtypeStruct((128, CELLS), BF16),
             jax.ShapeDtypeStruct((pack_rows, 128), BF16),
         ),
-        in_specs=[vmem] * 11,
+        in_specs=[vmem] * 13,
         out_specs=(vmem, vmem),
         scratch_shapes=[
+            pltpu.VMEM((4, 64, CELLS), BF16),
+            pltpu.VMEM((512, 128), BF16),
             pltpu.VMEM((2, 64, CELLS), BF16),
             pltpu.VMEM((2, 128, CELLS), BF16),
             pltpu.VMEM((2, 64, CELLS), BF16),
@@ -425,23 +469,29 @@
         ),
         name="network",
     )(
-        phased, cotangent.reshape(128, CELLS), jnp.asarray(selection(), BF16), w1,
+        volume.reshape(16, 16 * CELLS), cotangent.reshape(128, CELLS),
+        jnp.asarray(selection(), BF16), jnp.asarray(phase_spread(), BF16),
+        jnp.asarray(plane_order(), BF16), w1,
         b_first[:, None], w2, b_second[:, None], w3, b_third[:, None], w2f, w3f,
     )
 
     chunk = pack_rows // samples
-    summed = pl.pallas_call(
+    k1, b1, k2, b2, k3, b3 = pl.pallas_call(
         functools.partial(sum_kernel, samples, slabs),
-        out_shape=jax.ShapeDtypeStruct((pack_rows, 128), F32),
+        out_shape=tuple(
+            jax.ShapeDtypeStruct(shape, F32)
+            for shape in ((108, 32), (1, 32), (864, 64), (1, 64), (1728, 128), (1, 128))
+        ),
         in_specs=[vmem],
-        out_specs=vmem,
+        out_specs=(vmem,) * 6,
         scratch_shapes=[
             pltpu.VMEM((samples, chunk, 128), BF16),
             pltpu.VMEM((slabs, chunk // slabs, 128), BF16),
             pltpu.VMEM((chunk, 128), BF16),
             pltpu.VMEM((pack_rows, 128), BF16),
+            pltpu.VMEM((512, 32), F32),
         ]
-        + [pltpu.SemaphoreType.DMA((n,)) for n in (samples, samples, slabs, slabs) * 1]
+        + [pltpu.SemaphoreType.DMA((n,)) for n in (samples, samples, slabs, slabs)]
         + [pltpu.SemaphoreType.DMA((n,)) for n in (slabs, slabs, samples, samples)],
         compiler_params=pltpu.CompilerParams(
             collective_id=1, has_side_effects=True, vmem_limit_bytes=32 * 2**20
@@ -449,23 +499,14 @@
         name="sum_all",
     )(pack)
 
-    kernel_third = summed[:ROW_B3].reshape(27, 64, 128)
-    bias_third = summed[ROW_B3]
-    grad2 = summed[ROW_G2:ROW_B2]
-    kernel_second = jnp.concatenate([grad2[:, :64], grad2[:, 64:]], axis=0).reshape(27, 32, 64)
-    bias_second = summed[ROW_B2, :64]
-    grad1 = summed[ROW_G1:ROW_B1].reshape(4, 32, 128).transpose(1, 0, 2).reshape(32, 512)
-    grad1 = grad1[:, : 3 * PLANE].reshape(32, 3, 6, 6, 4)[:, :, :3, :3, :]
-    kernel_first = grad1.transpose(1, 2, 3, 4, 0).reshape(27, 4, 32)
-    bias_first = summed[ROW_B1:ROWS, 0]
     return (
         features.reshape(128, 1, 1, CELLS),
-        kernel_first,
-        bias_first,
-        kernel_second,
-        bias_second,
-        kernel_third,
-        bias_third,
+        k1.reshape(27, 4, 32),
+        b1.reshape(32),
+        k2.reshape(27, 32, 64),
+        b2.reshape(64),
+        k3.reshape(27, 64, 128),
+        b3.reshape(128),
     )
 
 

time: 92.1 us -> 66.7 us (0.72)
  local copies, waits for them, and re-layouts: 36.4 us -> 10.3 us
  Pallas kernels: 53.8 us -> 55.4 us
    transpose x1 -> x0, local copies, waits for them, and re-layouts: 16.3 us -> none  [per_device(): volume.reshape(4, 4, SY, 4, SX, 4).transpose(1, 3, 5, 0, 2, 4)]
    reshape x3 -> x2, local copies, waits for them, and re-layouts: 13.7 us -> 0.68 us  [the longest x1 0.64 us: per_device(): k1.reshape(27, 4, 32)]
    unnamed x18 -> x28, local copies, waits for them, and re-layouts: 0.69 us -> 8.47 us
    slice x6 -> x0, local copies, waits for them, and re-layouts: 2.47 us -> none  [the longest x1 0.97 us: per_device(): kernel_third = summed[:ROW_B3].reshape(27, 64, 128)]
    pallas_call x1, Pallas kernels: 21.3 us -> 22.7 us  [per_device(): pl.pallas_call(functools.partial(network_kernel, slabs), out_shape=(jax.S...]
    reshape x1, local copies, waits for them, and re-layouts: 1.11 us -> 0.05 us  [per_device(): w3f = w_third.transpose(1, 0, 2).reshape(64, 27 * 128)]
    squeeze x2 -> x0, local copies, waits for them, and re-layouts: 1.02 us -> none  [the longest x1 0.51 us: per_device(): bias_third = summed[ROW_B3]]
where the time goes in v2:
time: 66.7 us; the launch traced here: 66.5 us
  Pallas kernels  55.4 us (83%)
  local copies, waits for them, and re-layouts  10.3 us (15%)
  between operations  0.76 us (1%)
    pallas_call x1, Pallas kernels, per_device(): pl.pallas_call(functools.partial(sum_kernel, samples, slabs), out_shape=t...  32.7 us
    pallas_call x1, Pallas kernels, per_device(): pl.pallas_call(functools.partial(network_kernel, slabs), out_shape=(jax.S...  22.7 us
    unnamed x28, local copies, waits for them, and re-layouts  8.47 us

profile of v2, /device:TPU:1, one launch (start us, length us, event | category | flops | bytes accessed | tf_op | source)
XLA Modules:
  0.0 66.5 jit_solution(6461720034439728955)
XLA Ops:
  0.6 0.0 copy-start.10
  0.6 0.6 copy-done.10
  1.3 0.0 copy-start.8
  1.3 0.1 copy.31.b1_ref
  1.4 0.6 copy-done.8
  1.9 0.0 copy-start.9
  1.9 0.0 copy-start.7
  1.9 0.1 copy.32.b2_ref
  2.0 0.6 copy-done.9
  2.6 0.0 copy-start.5
  2.6 0.1 copy.33.b3_ref
  2.7 0.0 copy-done.7
  2.8 0.1 copy.26
  2.9 0.7 %copy-done.5 = bf16[27,32,64]{2,1,0:T(8,128)(2,1)S(1)} copy-done((bf16[27,32,64]{2,1,0:T(8,128)(2,1)S(1)}, bf16[27,32,64]{2,1,0:T(8,128)(2,1)}, u32[]{:S(2)}) %copy-start.5) | copy-done | bytes 110616
  3.5 0.0 copy-start.6
  3.5 0.1 copy.27
  3.7 0.8 %copy-done.6 = bf16[4,1,4,4096]{3,2,1,0:T(4,128)(2,1)S(1)} copy-done((bf16[4,1,4,4096]{3,2,1,0:T(4,128)(2,1)S(1)}, bf16[4,1,4,4096]{3,2,1,0:T(4,128)(2,1)}, u32[]{:S(2)}) %copy-start.6) | copy-done | bytes 131096
  4.5 0.0 copy-start.4
  4.5 0.1 copy.29
  4.6 0.0 copy-start
  4.6 0.2 reshape.67.w2f_ref
  4.9 0.6 copy-done.4
  5.5 0.1 copy_bitcast_fusion.w3f_ref
  5.6 0.0 copy-start.1
  5.6 0.0 copy-start.2
  5.6 0.0 copy-start.3
  5.6 0.2 copy.28
  5.8 0.1 copy-done
  5.9 0.7 copy-done.1
  6.5 0.0 copy-done.2
  6.6 0.0 copy-done.3
  6.6 22.7 %network.1 = (bf16[128,256]{1,0:T(8,128)(2,1)S(1)}, bf16[2560,128]{1,0:T(8,128)(2,1)S(1)}) custom-call(bf16[16,4096]{1,0:T(8,128)(2,1)S(1)} %reshape.61.vol_ref, bf16[128,256]{1,0:T(8,128)(2,1)S(1)} %bitcast.28, bf16[144,288]{1,0:T(8,128)(2,1)S(1)} %copy-done.2, bf16[128,4096]{1,0:T(8,128)(2,1)S(1)} %copy-done, bf16[256,256]{1,0:T(8,128)(2,1)S(1)} %copy-done.1, ...), custom_call_target="tpu_custom_call" | custom-call | tf_op jit(solution)/shard_map/network/pallas_call | solution.py:435
  29.3 32.7 %sum_all.1 = (f32[108,32]{1,0:T(8,128)S(1)}, f32[1,32]{1,0:T(1,128)S(1)}, f32[864,64]{1,0:T(8,128)S(1)}, f32[1,64]{1,0:T(1,128)S(1)}, f32[1728,128]{1,0:T(8,128)S(1)}, /*index=5*/f32[1,128]{1,0:T(1,128)S(1)}) custom-call(bf16[2560,128]{1,0:T(8,128)(2,1)S(1)} %get-tuple-element.16.pack_ref), custom_call_target="tpu_custom_call" | custom-call | tf_op jit(solution)/shard_map/sum_all/pallas_call | solution.py:479
  62.0 0.6 reshape.70
  62.6 0.6 copy.42
  63.3 0.5 copy.43
  63.8 0.8 %copy.44 = f32[27,32,64]{2,1,0:T(8,128)} copy(f32[27,32,64]{2,1,0:T(8,128)S(1)} %bitcast.27) | data formatting | bytes 442368
  64.5 0.5 copy.45
  65.0 0.9 %copy.46 = f32[27,64,128]{2,1,0:T(8,128)} copy(f32[27,64,128]{2,1,0:T(8,128)S(1)} %bitcast.25) | data formatting | bytes 1769472
  66.0 0.5 copy.47
  (3 shorter events, 0.1 us)
Async XLA Ops:
  0.6 0.7 copy-start.10
  1.3 0.7 copy-start.8
  1.9 0.7 copy-start.9
  1.9 0.8 %copy-start.7 = (bf16[27,4,32]{2,1,0:T(4,128)(2,1)S(1)}, bf16[27,4,32]{2,1,0:T(4,128)(2,1)}, u32[]{:S(2)}) copy-start(bf16[27,4,32]{2,1,0:T(4,128)(2,1)} %param.13) | copy-start | bytes 20740
  2.6 0.9 %copy-start.5 = (bf16[27,32,64]{2,1,0:T(8,128)(2,1)S(1)}, bf16[27,32,64]{2,1,0:T(8,128)(2,1)}, u32[]{:S(2)}) copy-start(bf16[27,32,64]{2,1,0:T(8,128)(2,1)} %param.15) | copy-start | bytes 331780
  3.5 0.9 %copy-start.6 = (bf16[4,1,4,4096]{3,2,1,0:T(4,128)(2,1)S(1)}, bf16[4,1,4,4096]{3,2,1,0:T(4,128)(2,1)}, u32[]{:S(2)}) copy-start(bf16[4,1,4,4096]{3,2,1,0:T(4,128)(2,1)} %param.11) | copy-start | bytes 393220
  4.5 1.0 %copy-start.4 = (bf16[27,64,128]{2,1,0:T(8,128)(2,1)S(1)}, bf16[27,64,128]{2,1,0:T(8,128)(2,1)}, u32[]{:S(2)}) copy-start(bf16[27,64,128]{2,1,0:T(8,128)(2,1)} %param.17) | copy-start | bytes 1327108
  4.6 1.3 %copy-start = (bf16[128,4096]{1,0:T(8,128)(2,1)S(1)}, bf16[128,4096]{1,0:T(8,128)(2,1)}, u32[]{:S(2)}) copy-start(bf16[128,4096]{1,0:T(8,128)(2,1)} %constant.11.clone.spread_ref) | copy-start | bytes 3145732
  5.6 1.0 %copy-start.1 = (bf16[256,256]{1,0:T(8,128)(2,1)S(1)}, bf16[256,256]{1,0:T(8,128)(2,1)}, u32[]{:S(2)}) copy-start(bf16[256,256]{1,0:T(8,128)(2,1)} %constant.12.clone.order_ref) | copy-start | bytes 393220
  5.6 1.0 %copy-start.2 = (bf16[144,288]{1,0:T(8,128)(2,1)S(1)}, bf16[144,288]{1,0:T(8,128)(2,1)}, u32[]{:S(2)}) copy-start(bf16[144,288]{1,0:T(8,128)(2,1)} %constant.10.clone.sel_ref) | copy-start | bytes 248836
  5.6 1.0 %copy-start.3 = (bf16[128,1,1,256]{3,0,2,1:T(8,128)(2,1)S(1)}, bf16[128,1,1,256]{3,0,2,1:T(8,128)(2,1)}, u32[]{:S(2)}) copy-start(bf16[128,1,1,256]{3,0,2,1:T(8,128)(2,1)} %param.12) | copy-start | bytes 196612
